TPU v7x, 32 devices: a whole 2x2x4 slice. The times are simulated.
32 devices in a mesh: dp: 4 (over y, x), expert: 8 (over z, core).
Axes of the slice: x: 2, y: 2, z: 4, core: 2. Of those that a mesh axis runs over, the one named last changes fastest.
Arguments:
- tokens: bfloat16 [4096, 3584], P(('dp', 'expert')), may hold values from -6 to 6
- cotangent: bfloat16 [4096, 3584], P(('dp', 'expert')), may hold values from -0.375 to 0.375
- gate_scale: float32 [4096], P(('dp', 'expert')), may hold values from 0.2 to 1
- expert_index: int32 [4096], P(('dp', 'expert')), may hold values from 0 to 7, as said below
- hot_index: int32 [8], replicated, may hold values from 0 to 7, as said below
- w_gate: bfloat16 [8, 3584, 1024], P('expert', None, 'dp'), may hold values from -0.09375 to 0.09375
- w_up: bfloat16 [8, 3584, 1024], P('expert', None, 'dp'), may hold values from -0.09375 to 0.09375
- w_down: bfloat16 [8, 1024, 3584], P('expert', 'dp'), may hold values from -0.1875 to 0.1875
Outputs:
- grad_gate: bfloat16 [8, 3584, 1024], P('expert', None, 'dp')
- grad_up: bfloat16 [8, 3584, 1024], P('expert', None, 'dp')
- grad_down: bfloat16 [8, 1024, 3584], P('expert', 'dp')
- hot_grads: bfloat16 [1, 3584, 3, 1024], P(None, 'expert', None, 'dp')
Inputs may be any that keep to these rules, and one draw needn't show every extreme that they name: `expert_index`: among the 128 tokens of one device (aligned blocks of rows), at most 24 are routed to any one expert other than hot_index[0], and from 24 to 48 to hot_index[0]. In every draw each group of devices sharing a dp index has an expert that receives exactly 24 tokens from each of its devices, and some devices route exactly 48 tokens to hot_index[0]. `hot_index`: A permutation of the 8 experts; its first entry is the replicated expert, to which every device routes at least as many tokens as to any other expert.
All inputs are finite; a program needn't handle non-finite values.
Results may differ from a plain program's by a relative error of at most 0.0058.
Values may be sent and summed in bfloat16 or wider, within the bound.
No kernel may reach another device: no remote copies, remote signals or barrier semaphores. Data moves between devices by JAX's collectives and lax.ppermute only.
A program may use at most 128 MiB of HBM per device.

v0:
```python
import jax
import jax.numpy as jnp
from jax import lax
from jax.sharding import PartitionSpec as P

CONTRACT_ROWS = (((0,), (0,)), ((), ()))


def spread(block, axis, source):
    block = jnp.where(lax.axis_index(axis) == source, block, jnp.zeros_like(block))
    return lax.psum(block, axis)


def expert_terms(row_tokens, row_grads, gate_matrix, up_matrix, down_matrix):
    pre_gate = jnp.dot(row_tokens, gate_matrix, preferred_element_type=jnp.float32)
    pre_up = jnp.dot(row_tokens, up_matrix, preferred_element_type=jnp.float32)
    hidden_back = lax.dot_general(
        row_grads, down_matrix, (((1,), (1,)), ((), ())), preferred_element_type=jnp.float32
    )
    sigmoid_gate = jax.nn.sigmoid(pre_gate)
    activated = pre_gate * sigmoid_gate
    hidden = (activated * pre_up).astype(jnp.bfloat16)
    gate_grad = (
        hidden_back * pre_up * sigmoid_gate * (1.0 + pre_gate * (1.0 - sigmoid_gate))
    ).astype(jnp.bfloat16)
    up_grad = (hidden_back * activated).astype(jnp.bfloat16)
    return (hidden, gate_grad, up_grad)


def column_sum(left, right):
    return lax.dot_general(left, right, CONTRACT_ROWS, preferred_element_type=jnp.float32)


def route_rows(selector, values):
    return jnp.dot(selector, values, preferred_element_type=jnp.float32).astype(jnp.bfloat16)


def on_device(tokens, cotangent, gate_scale, expert_index, hot_index, w_gate, w_up, w_down):
    tok_rows, feature_width = tokens.shape
    experts = lax.axis_size("expert")
    capacity = 3 * tok_rows // (2 * experts)
    hot_capacity = 2 * capacity
    hot_expert = hot_index[0]
    route_grad = (gate_scale[:, None] * cotangent.astype(jnp.float32)).astype(jnp.bfloat16)
    is_hot = expert_index == hot_expert
    not_hot = jnp.logical_not(is_hot)
    owners = lax.broadcasted_iota(jnp.int32, (tok_rows, experts), 1)
    member = ((expert_index[:, None] == owners) & not_hot[:, None]).astype(jnp.int32)
    bucket_place = jnp.sum((jnp.cumsum(member, axis=0) - 1) * member, axis=1)
    slot_index = expert_index * capacity + bucket_place
    slot_grid = lax.broadcasted_iota(jnp.int32, (experts * capacity, tok_rows), 0)
    cold_map = ((slot_grid == slot_index[None, :]) & not_hot[None, :]).astype(jnp.bfloat16)
    hot_place = jnp.cumsum(is_hot.astype(jnp.int32)) - 1
    hot_grid = lax.broadcasted_iota(jnp.int32, (hot_capacity, tok_rows), 0)
    hot_map = ((hot_grid == hot_place[None, :]) & is_hot[None, :]).astype(jnp.bfloat16)
    send_tokens = route_rows(cold_map, tokens).reshape(experts, capacity, feature_width)
    send_grads = route_rows(cold_map, route_grad).reshape(experts, capacity, feature_width)
    own_hot_tokens = route_rows(hot_map, tokens)
    own_hot_grads = route_rows(hot_map, route_grad)
    arrived_tokens, arrived_grads = (
        lax.all_to_all(send_tokens, "expert", split_axis=0, concat_axis=0, tiled=True),
        lax.all_to_all(send_grads, "expert", split_axis=0, concat_axis=0, tiled=True),
    )
    cold_tokens, cold_grads, hot_tokens, hot_row_grads = (
        lax.all_gather(
            arrived_tokens.reshape(experts * capacity, feature_width), "dp", axis=0, tiled=True
        ),
        lax.all_gather(
            arrived_grads.reshape(experts * capacity, feature_width), "dp", axis=0, tiled=True
        ),
        lax.all_gather(own_hot_tokens, "dp", axis=0, tiled=True),
        lax.all_gather(own_hot_grads, "dp", axis=0, tiled=True),
    )
    shadow_gate, shadow_up, shadow_down = (
        spread(w_gate[0], "expert", hot_expert),
        spread(w_up[0], "expert", hot_expert),
        spread(w_down[0], "expert", hot_expert),
    )
    hidden, gate_grad, up_grad = expert_terms(
        cold_tokens, cold_grads, w_gate[0], w_up[0], w_down[0]
    )
    grad_gate = column_sum(cold_tokens, gate_grad).astype(jnp.bfloat16)
    grad_up = column_sum(cold_tokens, up_grad).astype(jnp.bfloat16)
    grad_down = column_sum(hidden, cold_grads).astype(jnp.bfloat16)
    hot_hidden, hot_gate_grad, hot_up_grad = expert_terms(
        hot_tokens, hot_row_grads, shadow_gate, shadow_up, shadow_down
    )
    gate_part = column_sum(hot_tokens, hot_gate_grad)
    up_part = column_sum(hot_tokens, hot_up_grad)
    down_part = column_sum(hot_row_grads, hot_hidden)
    owned_part = lax.psum_scatter(
        jnp.stack([gate_part, up_part, down_part], axis=1),
        "expert",
        scatter_dimension=0,
        tiled=True,
    )
    hot_grads = owned_part.astype(jnp.bfloat16)[None]
    return (grad_gate[None], grad_up[None], grad_down[None], hot_grads)


def solution(mesh):
    placed = (
        P(("dp", "expert"), None),
        P(("dp", "expert"), None),
        P(("dp", "expert")),
        P(("dp", "expert")),
        P(),
        P("expert", None, "dp"),
        P("expert", None, "dp"),
        P("expert", "dp", None),
    )
    return jax.shard_map(
        on_device,
        mesh=mesh,
        in_specs=placed,
        out_specs=(
            P("expert", None, "dp"),
            P("expert", None, "dp"),
            P("expert", "dp", None),
            P(None, "expert", None, "dp"),
        ),
        check_vma=False,
    )
```

profile of v0, /device:TPU:0, one launch (start us, length us, event | category | flops | bytes accessed | tf_op | source)
XLA Modules:
  0.0 340.6 jit_solution(2158308090245639226)
XLA Ops:
  8.1 1.5 convert_bitcast_fusion.1
  9.9 1.0 convolution_convert_fusion.6
  11.1 1.4 bitcast_select_fusion.2
  13.8 2.1 bitcast_select_fusion
  17.0 1.7 convolution_convert_fusion.4
  18.7 6.5 %all-to-all-start = ((bf16[8,24,3584]{2,1,0:T(8,128)(2,1)}), bf16[8,24,3584]{2,1,0:T(8,128)(2,1)S(1)}, u32[]{:S(2)}, u32[]{:S(2)}) async-start(bf16[8,24,3584]{2,1,0:T(8,128)(2,1)} %bitcast.53), calls=%async_computation | async-start | bytes 2752512 | tf_op jit(solution)/shard_map/all_to_all | solution.py:61
  25.2 1.1 convolution_convert_fusion.5
  26.4 46.7 %all-to-all-done = bf16[8,24,3584]{2,1,0:T(8,128)(2,1)S(1)} async-done(((bf16[8,24,3584]{2,1,0:T(8,128)(2,1)}), bf16[8,24,3584]{2,1,0:T(8,128)(2,1)S(1)}, u32[]{:S(2)}, u32[]{:S(2)}) %all-to-all-start) | async-done | bytes 1376288 | tf_op jit(solution)/shard_map/all_to_all | solution.py:61
  73.1 1.1 copy-done.4
  74.8 52.2 %all_to_all.10 = bf16[8,24,3584]{2,1,0:T(8,128)(2,1)} all-to-all(bf16[8,24,3584]{2,1,0:T(8,128)(2,1)S(1)} %bitcast.54), channel_id=1, replica_groups=mesh['dp'=4,'expert'=8] {'expert'}, dimensions={0} | all-to-all | bytes 2752512 | tf_op jit(solution)/shard_map/all_to_all | solution.py:62
  127.3 71.2 %all-reduce.3.cloned.1.call-done = (bf16[3584,256]{1,0:T(8,128)(2,1)}, bf16[3584,256]{1,0:T(8,128)(2,1)}, bf16[256,3584]{1,0:T(8,128)(2,1)}) async-done(((bf16[3584,256]{1,0:T(8,128)(2,1)}, bf16[3584,256]{1,0:T(8,128)(2,1)}, bf16[256,3584]{1,0:T(8,128)(2,1)}), (bf16[3584,256]{1,0:T(8,128)(2,1)}, bf16[3584,256]{1,0:T(8,128)(2,1)}, bf16[256,3584]{1,0:T(8,128)(2,1)})) %all-reduce.3.cloned.1.call-update) | async-done | bytes 5505040 | tf_op jit(solution)/shard_map/psum | solution.py:11
  198.5 2.4 fusion.41
  201.0 2.7 fusion.39
  207.3 2.6 convolution_bitcast_fusion.2
  209.9 6.9 %pad_maximum_fusion = f32[3584,3,256]{2,0,1:T(8,128)} fusion(f32[3584,1,256]{2,0,1:T(8,128)S(1)} %convolution_bitcast_fusion, f32[3584,1,256]{2,0,1:T(8,128)S(1)} %convolution_bitcast_fusion.1, f32[3584,1,256]{2,0,1:T(8,128)} %convolution_bitcast_fusion.2), kind=kLoop, calls=%fused_computation | loop fusion | flops 5505024 | bytes 22020096 | tf_op jit(solution)/shard_map/stack | solution.py:92
  216.9 1.4 copy-done.10
  218.4 4.3 %fusion.3 = f32[768,256]{1,0:T(8,128)S(1)} fusion(bf16[768,3584]{1,0:T(8,128)(2,1)} %all-gather.5.cloned.1.call-done, bf16[1,3584,256]{2,1,0:T(8,128)(2,1)S(1)} %copy-done.10), kind=kOutput, calls=%fused_computation.15 | convolution fusion | flops 1409286144 | bytes 8126464 | tf_op jit(solution)/shard_map/dot_general | solution.py:15
  223.2 1.6 fusion.5
  224.9 4.3 %fusion.7 = f32[768,256]{1,0:T(8,128)S(1)} fusion(bf16[768,3584]{1,0:T(8,128)(2,1)} %all-gather.7.cloned.1.call-done, bf16[1,256,3584]{2,1,0:T(8,128)(2,1)S(1)} %copy-done.7), kind=kOutput, calls=%fused_computation.21 | convolution fusion | flops 1409286144 | bytes 8126464 | tf_op jit(solution)/shard_map/dot_general | solution.py:17
  229.3 3.0 fusion.2
  232.3 3.1 fusion.1
  235.4 3.2 fusion
  238.6 92.6 %reduce-scatter.2.cloned.1.call-done = f32[448,3,256]{2,0,1:T(8,128)} async-done(((f32[3584,3,256]{2,0,1:T(8,128)}), f32[448,3,256]{2,0,1:T(8,128)}) %reduce-scatter.2.cloned.1.call-update) | async-done | bytes 1376272 | tf_op jit(solution)/shard_map/reduce_scatter | solution.py:91
  331.2 2.3 convert_bitcast_fusion
  (71 shorter events, 8.3 us)
Async XLA Ops:
  8.0 1.9 copy-start
  8.0 3.0 copy-start.15
  8.0 3.1 copy-start.6
  8.0 119.2 %all-gather.9.cloned.1.call-start = ((), (), s32[]{:S(2)}) async-start(), calls=%async_computation.5 | async-start | bytes 1720320 | tf_op jit(solution)/shard_map/all_gather | solution.py:71
  11.0 187.5 %all-reduce.3.cloned.1.call-start = ((), (), s32[]{:S(2)}) async-start(), calls=%async_computation.8 | async-start | bytes 11010048 | tf_op jit(solution)/shard_map/psum | solution.py:11
  11.1 2.2 copy-start.9
  11.1 2.7 copy-start.11
  18.7 6.5 %copy-start.5 = (bf16[128,3584]{1,0:T(8,128)(2,1)S(1)}, bf16[128,3584]{1,0:T(8,128)(2,1)}, u32[]{:S(2)}) copy-start(bf16[128,3584]{1,0:T(8,128)(2,1)} %param.9) | copy-start | bytes 2752516
  18.7 6.5 %copy-start.14 = (f32[128]{0:T(128)S(1)}, f32[128]{0:T(128)}, u32[]{:S(2)}) copy-start(f32[128]{0:T(128)} %param.10) | copy-start | bytes 1540
  18.7 54.4 %all-to-all-start = ((bf16[8,24,3584]{2,1,0:T(8,128)(2,1)}), bf16[8,24,3584]{2,1,0:T(8,128)(2,1)S(1)}, u32[]{:S(2)}, u32[]{:S(2)}) async-start(bf16[8,24,3584]{2,1,0:T(8,128)(2,1)} %bitcast.53), calls=%async_computation | async-start | bytes 2752512 | tf_op jit(solution)/shard_map/all_to_all | solution.py:61
  25.1 175.9 %all-gather.11.cloned.1.call-start = ((), (), s32[]{:S(2)}) async-start(), calls=%async_computation.6 | async-start | bytes 1720320 | tf_op jit(solution)/shard_map/all_gather | solution.py:72
  26.3 190.6 %all-gather.5.cloned.1.call-start = ((), (), s32[]{:S(2)}) async-start(), calls=%async_computation.3 | async-start | bytes 6881280 | tf_op jit(solution)/shard_map/all_gather | solution.py:65
  74.2 150.6 %all-gather.7.cloned.1.call-start = ((), (), s32[]{:S(2)}) async-start(), calls=%async_computation.4 | async-start | bytes 6881280 | tf_op jit(solution)/shard_map/all_gather | solution.py:68
  127.0 204.2 %reduce-scatter.2.cloned.1.call-start = ((), (), s32[]{:S(2)}) async-start(), calls=%async_computation.7 | async-start | bytes 12386304 | tf_op jit(solution)/shard_map/reduce_scatter | solution.py:91
  201.0 2.8 copy-start.2
  218.4 4.3 %copy-start.12 = (bf16[1,3584,256]{2,1,0:T(8,128)(2,1)S(1)}, bf16[1,3584,256]{2,1,0:T(8,128)(2,1)}, u32[]{:S(2)}) copy-start(bf16[1,3584,256]{2,1,0:T(8,128)(2,1)} %param.14) | copy-start | bytes 5505028
  218.4 4.8 %copy-start.16 = (bf16[768,3584]{1,0:T(8,128)(2,1)S(1)}, bf16[768,3584]{1,0:T(8,128)(2,1)}, u32[]{:S(2)}) copy-start(bf16[768,3584]{1,0:T(8,128)(2,1)} %all-gather.5.cloned.1.call-done) | copy-start | bytes 16515076
  223.2 1.8 copy-start.7
  224.8 4.5 %copy-start.18 = (f32[768,256]{1,0:T(8,128)}, f32[768,256]{1,0:T(8,128)S(1)}, u32[]{:S(2)}) copy-start(f32[768,256]{1,0:T(8,128)S(1)} %fusion.5) | copy-start | bytes 2359300
  224.9 4.4 %copy-start.17 = (bf16[768,3584]{1,0:T(8,128)(2,1)S(1)}, bf16[768,3584]{1,0:T(8,128)(2,1)}, u32[]{:S(2)}) copy-start(bf16[768,3584]{1,0:T(8,128)(2,1)} %all-gather.7.cloned.1.call-done) | copy-start | bytes 16515076
  224.9 7.3 %slice-start = ((s8[5505024]{0:T(1024)(128)(4,1)}), s8[4194304]{0:T(1024)(128)(4,1)S(1)}, s32[]{:S(2)}) async-start(s8[5505024]{0:T(1024)(128)(4,1)} %bitcast.57), calls=%async_computation.9 | async-start | bytes 8388608
  229.3 3.0 slice-start.1
  232.3 3.1 copy-start.19
  235.4 98.1 %copy-start.1 = (bf16[128,3584]{1,0:T(8,128)(2,1)S(1)}, bf16[128,3584]{1,0:T(8,128)(2,1)}, u32[]{:S(2)}) copy-start(bf16[128,3584]{1,0:T(8,128)(2,1)} %param.8) | copy-start | bytes 2752516
  (5 other events, 6.1 us)
Sparse Core Ops, SparseCore 0:
  11.1 32.0 all-gather.8
  45.6 29.3 all-gather.10
  76.8 63.5 all-gather.4
  142.2 63.6 all-gather.6
Sparse Core Ops, SparseCore 1:
  16.0 182.5 all-reduce.2
  217.0 114.2 reduce-scatter.1
where the time goes:
time: 341 us
  waiting for transfers between devices  211 us (62%)
  blocking collectives  52.2 us (15%)
  matrix products  33.6 us (10%)
  between operations  15.5 us (5%)
  other arithmetic  14.8 us (4%)
  local copies, waits for them, and re-layouts  6.88 us (2%)
  starting transfers between devices  6.88 us (2%)
    reduce_scatter x1, waiting for transfers between devices, on_device(): lax.psum_scatter(jnp.stack([gate_part, up_part, down_part], axis=1), 'exp...  92.6 us
    psum x1, waiting for transfers between devices, spread(): return lax.psum(block, axis)  71.2 us
    all_to_all x1, blocking collectives, on_device(): lax.all_to_all(send_grads, 'expert', split_axis=0, concat_axis=0, tiled=T...  52.2 us
    all_to_all x1, waiting for transfers between devices, on_device(): lax.all_to_all(send_tokens, 'expert', split_axis=0, concat_axis=0, tiled=...  46.7 us
    dot_general x6, matrix products, column_sum(): lax.dot_general(left, right, CONTRACT_ROWS, preferred_element_type=jnp.fl...  13.3 us
    dot_general x2, matrix products, expert_terms(): lax.dot_general(row_grads, down_matrix, (((1,), (1,)), ((), ())), preferr...  7.09 us
    another operation x1, other arithmetic, on_device(): jnp.stack([gate_part, up_part, down_part], axis=1)  6.94 us
  transfers between devices with their start and end apart: 7, of which 3 were waited for; matrix products, arithmetic and copies ran while one was open for 13% of the time, Pallas kernels for 0%

commit v1 on v0

--- a/solution.py
+++ b/solution.py
@@ -1,6 +1,10 @@
+import functools
+
 import jax
 import jax.numpy as jnp
 from jax import lax
+from jax.experimental import pallas as pl
+from jax.experimental.pallas import tpu as pltpu
 from jax.sharding import PartitionSpec as P
 
 CONTRACT_ROWS = (((0,), (0,)), ((), ()))
@@ -35,7 +39,7 @@
     return jnp.dot(selector, values, preferred_element_type=jnp.float32).astype(jnp.bfloat16)
 
 
-def on_device(tokens, cotangent, gate_scale, expert_index, hot_index, w_gate, w_up, w_down):
+def on_large_mesh(tokens, cotangent, gate_scale, expert_index, hot_index, w_gate, w_up, w_down):
     tok_rows, feature_width = tokens.shape
     experts = lax.axis_size("expert")
     capacity = 3 * tok_rows // (2 * experts)
@@ -98,6 +102,386 @@
     return (grad_gate[None], grad_up[None], grad_down[None], hot_grads)
 
 
+ANYWHERE = pl.BlockSpec(memory_space=pl.ANY)
+VMEM_LIMIT = 56 * 2**20
+
+
+def together(*arrays):
+    return pl.pallas_call(
+        lambda *refs: None,
+        out_shape=[jax.ShapeDtypeStruct(a.shape, a.dtype) for a in arrays],
+        in_specs=[ANYWHERE] * len(arrays),
+        out_specs=[ANYWHERE] * len(arrays),
+        input_output_aliases={i: i for i in range(len(arrays))},
+        name="together",
+    )(*arrays)
+
+
+def divisor(size, most, unit):
+    return max(d for d in range(unit, most + 1, unit) if size % d == 0)
+
+
+def terms_kernel(plan, hot, chips, n_sources, block_rows, block_columns, *refs):
+    flags, mine, theirs = refs[0], refs[1 : 1 + n_sources], refs[1 + n_sources : 1 + 2 * n_sources]
+    gate_ref, up_ref, down_ref = refs[1 + 2 * n_sources : 4 + 2 * n_sources]
+    rest = refs[4 + 2 * n_sources :]
+    n_out = 6 if hot else 3
+    outs = rest[:n_out]
+    tok, grd, gate_w, up_w, down_w, gate_up_t, hidden_t, res_a, res_b, res_c, in_sem, w_sem, out_sem = rest[n_out:]
+    rows, width = tok.shape
+    hidden_width = gate_w.shape[1]
+    core = flags[0]
+
+    def copies(choice, core_value):
+        at, result = 0, []
+        for k, (source, first, count) in enumerate(plan[choice]):
+            own, other = (mine, theirs) if core_value == 0 else (theirs, mine)
+            for kind, (ref, buffer) in enumerate(((own, tok), (other, grd))):
+                result.append(
+                    pltpu.make_async_copy(
+                        ref[source].at[pl.ds(first, count)],
+                        buffer.at[pl.ds(at, count)],
+                        in_sem.at[2 * k + kind],
+                    )
+                )
+            at += count
+        return result
+
+    def output(wanted):
+        column_blocks = width // block_columns
+        if not hot:
+            for i in range(column_blocks):
+                span = pl.ds(i * block_columns, block_columns)
+                yield pltpu.make_async_copy(res_a.at[span], outs[0].at[span], out_sem.at[i])
+                yield pltpu.make_async_copy(
+                    res_b.at[span], outs[1].at[span], out_sem.at[column_blocks + i]
+                )
+            yield pltpu.make_async_copy(res_c, outs[2], out_sem.at[2 * column_blocks])
+            return
+        part = width // (2 * chips)
+        for q, res in enumerate((res_a, res_b, res_c)):
+            for z in range(chips):
+                for c in range(2):
+                    yield pltpu.make_async_copy(
+                        res.at[pl.ds((2 * z + c) * part, part)],
+                        outs[2 * q + (c != wanted)].at[z],
+                        out_sem.at[(q * chips + z) * 2 + c],
+                    )
+
+    def work():
+        weights = [
+            pltpu.make_async_copy(w, buffer, w_sem.at[i])
+            for i, (w, buffer) in enumerate(((gate_ref, gate_w), (up_ref, up_w), (down_ref, down_w)))
+        ]
+        for copy in weights:
+            copy.start()
+        for choice in range(len(plan)):
+            for core_value in range(2):
+
+                @pl.when((flags[2] == choice) & (core == core_value))
+                def _():
+                    for copy in copies(choice, core_value):
+                        copy.start()
+
+        for copy in weights:
+            copy.wait()
+        waits = copies(0, 0)
+        sizes = [count for _, _, count in plan[0]]
+        arrived = 0
+        for block in range(rows // block_rows):
+            while sum(sizes[:arrived]) < (block + 1) * block_rows:
+                waits[2 * arrived].wait()
+                waits[2 * arrived + 1].wait()
+                arrived += 1
+            span = pl.ds(block * block_rows, block_rows)
+            row_tokens, row_grads = tok[span, :], grd[span, :]
+            pre_gate = jnp.dot(row_tokens, gate_w[...], preferred_element_type=jnp.float32)
+            pre_up = jnp.dot(row_tokens, up_w[...], preferred_element_type=jnp.float32)
+            hidden_back = lax.dot_general(
+                row_grads, down_w[...], (((1,), (1,)), ((), ())), preferred_element_type=jnp.float32
+            )
+            sigmoid_gate = jax.nn.sigmoid(pre_gate)
+            activated = pre_gate * sigmoid_gate
+            hidden = activated * pre_up
+            gate_grad = hidden_back * pre_up * sigmoid_gate * (1.0 + pre_gate * (1.0 - sigmoid_gate))
+            up_grad = hidden_back * activated
+            hidden_t[:, span] = hidden.T.astype(jnp.bfloat16)
+            gate_up_t[pl.ds(0, hidden_width), span] = gate_grad.T.astype(jnp.bfloat16)
+            gate_up_t[pl.ds(hidden_width, hidden_width), span] = up_grad.T.astype(jnp.bfloat16)
+
+        def columns(i, carry):
+            span = pl.ds(pl.multiple_of(i * block_columns, block_columns), block_columns)
+            sums = jnp.dot(gate_up_t[...], tok[:, span], preferred_element_type=jnp.float32)
+            sums = sums.T.astype(jnp.bfloat16)
+            res_a[span, :] = sums[:, :hidden_width]
+            res_b[span, :] = sums[:, hidden_width:]
+            downs = jnp.dot(hidden_t[...], grd[:, span], preferred_element_type=jnp.float32)
+            if hot:
+                res_c[span, :] = downs.T.astype(jnp.bfloat16)
+            else:
+                res_c[:, span] = downs.astype(jnp.bfloat16)
+            return carry
+
+        lax.fori_loop(0, width // block_columns, columns, 0)
+
+    if hot:
+        for core_value in range(2):
+
+            @pl.when((flags[1] == 1) & (core == core_value))
+            def _():
+                if core_value == 0:
+                    work()
+                else:
+                    work()
+                sent = list(output(core_value))
+                for copy in sent:
+                    copy.start()
+                for copy in sent:
+                    copy.wait()
+
+    else:
+
+        @pl.when(flags[1] == 1)
+        def _():
+            work()
+
+        @pl.when(flags[1] == 0)
+        def _():
+            for res in (res_a, res_b, res_c):
+                res[...] = jnp.zeros_like(res)
+
+        sent = list(output(None))
+        for copy in sent:
+            copy.start()
+        for copy in sent:
+            copy.wait()
+
+
+def expert_call(flags, plan, hot, chips, mine, theirs, gate, up, down):
+    width, hidden_width = gate.shape
+    rows = sum(count for _, _, count in plan[0])
+    block_rows = divisor(rows, 384, 128)
+    block_columns = divisor(width, 512, 128)
+    part = width // (2 * chips)
+    if hot:
+        out_shape = [jax.ShapeDtypeStruct((chips, part, hidden_width), jnp.bfloat16)] * 6
+        n_out_copies = 6 * chips
+    else:
+        out_shape = [
+            jax.ShapeDtypeStruct((width, hidden_width), jnp.bfloat16),
+            jax.ShapeDtypeStruct((width, hidden_width), jnp.bfloat16),
+            jax.ShapeDtypeStruct((hidden_width, width), jnp.bfloat16),
+        ]
+        n_out_copies = 2 * (width // block_columns) + 1
+    last = (width, hidden_width) if hot else (hidden_width, width)
+    kernel = functools.partial(
+        terms_kernel, plan, hot, chips, len(mine), block_rows, block_columns
+    )
+    return pl.pallas_call(
+        kernel,
+        out_shape=out_shape,
+        in_specs=[pl.BlockSpec(memory_space=pltpu.SMEM)] + [ANYWHERE] * (2 * len(mine) + 3),
+        out_specs=[ANYWHERE] * len(out_shape),
+        scratch_shapes=[
+            pltpu.VMEM((rows, width), jnp.bfloat16),
+            pltpu.VMEM((rows, width), jnp.bfloat16),
+            pltpu.VMEM((width, hidden_width), jnp.bfloat16),
+            pltpu.VMEM((width, hidden_width), jnp.bfloat16),
+            pltpu.VMEM((hidden_width, width), jnp.bfloat16),
+            pltpu.VMEM((2 * hidden_width, rows), jnp.bfloat16),
+            pltpu.VMEM((hidden_width, rows), jnp.bfloat16),
+            pltpu.VMEM((width, hidden_width), jnp.bfloat16),
+            pltpu.VMEM((width, hidden_width), jnp.bfloat16),
+            pltpu.VMEM(last, jnp.bfloat16),
+            pltpu.SemaphoreType.DMA((2 * len(plan[0]),)),
+            pltpu.SemaphoreType.DMA((3,)),
+            pltpu.SemaphoreType.DMA((n_out_copies,)),
+        ],
+        compiler_params=pltpu.CompilerParams(vmem_limit_bytes=VMEM_LIMIT),
+        cost_estimate=pl.CostEstimate(
+            flops=12 * rows * width * hidden_width,
+            bytes_accessed=4 * rows * width + 12 * width * hidden_width,
+            transcendentals=rows * hidden_width,
+        ),
+        name="hot_terms" if hot else "cold_terms",
+    )(flags, *mine, *theirs, gate, up, down)
+
+
+def on_device(tokens, cotangent, gate_scale, expert_index, hot_index, w_gate, w_up, w_down):
+    tok_rows, width = tokens.shape
+    experts = lax.axis_size("expert")
+    dp = lax.axis_size("dp")
+    chips = experts // 2
+    capacity = 3 * tok_rows // (2 * experts)
+    if chips != 4 or dp != 4 or capacity % 8 != 0:
+        return on_large_mesh(
+            tokens, cotangent, gate_scale, expert_index, hot_index, w_gate, w_up, w_down
+        )
+    hot_expert = hot_index[0]
+    me = lax.axis_index("expert")
+    core, chip = me % 2, me // 2
+    flat = [(i, j) for i in range(dp) for j in range(experts)]
+
+    def place_of(i, j):
+        return i * experts + j
+
+    def swap(array):
+        return lax.ppermute(array, "expert", [(j, j ^ 1) for j in range(experts)])
+
+    def along(array, step):
+        return lax.ppermute(array, "expert", [(j, j ^ (2 * step)) for j in range(experts)])
+
+    def first_way(array):
+        pairs = [(place_of(i, j), place_of(i ^ (2 if j % 2 else 1), j)) for i, j in flat]
+        return lax.ppermute(array, ("dp", "expert"), pairs)
+
+    def second_way(array):
+        pairs = [(place_of(i, j), place_of(i ^ (1 if j % 2 else 2), j)) for i, j in flat]
+        return lax.ppermute(array, ("dp", "expert"), pairs)
+
+    route_grad = (gate_scale[:, None] * cotangent.astype(jnp.float32)).astype(jnp.bfloat16)
+    own = jnp.where(core == 0, tokens, route_grad)
+    other = jnp.where(core == 0, route_grad, tokens)
+    sibling, sibling_index = swap(other), swap(expert_index)
+    earlier = lax.broadcasted_iota(jnp.int32, (tok_rows, tok_rows), 1) < lax.broadcasted_iota(
+        jnp.int32, (tok_rows, tok_rows), 0
+    )
+
+    def places(index):
+        return jnp.sum(((index[:, None] == index[None, :]) & earlier).astype(jnp.int32), axis=1)
+
+    index = jnp.concatenate([expert_index, sibling_index])
+    place = jnp.concatenate([places(expert_index), places(sibling_index)])
+    holder = jnp.concatenate([jnp.full((tok_rows,), core), jnp.full((tok_rows,), 1 - core)])
+    values = jnp.concatenate([own, sibling], axis=0)
+    message = 2 * capacity
+    slots = lax.broadcasted_iota(jnp.int32, (message, 2 * tok_rows), 0)
+
+    def selector(kind, step):
+        target = chip ^ step
+        expert = jnp.where(hot_expert // 2 == target, hot_expert, 2 * target)
+        offset = 0
+        if kind == "second":
+            expert = expert ^ 1
+        elif kind == "rest":
+            expert, offset = hot_expert, capacity
+        taken = (index == expert) & (place >= offset) & (place < offset + capacity)
+        slot = place - offset + capacity * holder
+        return ((slots == slot[None, :]) & taken[None, :]).astype(jnp.bfloat16)
+
+    def rows(*wanted):
+        return route_rows(jnp.concatenate([selector(*w) for w in wanted], axis=0), values)
+
+    near_unit = rows(("first", 0), ("rest", 0))
+    sent = {k: [rows((k, s)) for s in range(1, chips)] for k in ("first", "rest", "second")}
+    own_second = rows(("second", 0))
+
+    near_1, side_1 = first_way(near_unit), second_way(near_unit)
+    got = [along(block, s) for s, block in enumerate(sent["first"], 1)]
+    first_unit = jnp.concatenate(got, axis=0)
+    near_unit, near_1, side_1, first_unit, *sent["rest"] = together(
+        near_unit, near_1, side_1, first_unit, *sent["rest"]
+    )
+    far_1 = second_way(near_1)
+    near_2, side_2 = first_way(first_unit), second_way(first_unit)
+    got = [along(block, s) for s, block in enumerate(sent["rest"], 1)]
+    swapped_1 = [swap(a) for a in (near_unit, side_1, near_1)]
+    rest_unit = jnp.concatenate(got, axis=0)
+    far_1, first_unit, near_2, side_2, rest_unit, *sent["second"] = together(
+        far_1, first_unit, near_2, side_2, rest_unit, *sent["second"]
+    )
+    far_2 = second_way(near_2)
+    near_3, side_3 = first_way(rest_unit), second_way(rest_unit)
+    got = [along(block, s) for s, block in enumerate(sent["second"], 1)]
+    swapped_1.append(swap(far_1))
+    swapped_2 = [swap(a) for a in (first_unit, side_2, near_2)]
+    second_unit = jnp.concatenate([own_second] + got, axis=0)
+    far_2, rest_unit, near_3, side_3, second_unit = together(
+        far_2, rest_unit, near_3, side_3, second_unit
+    )
+    far_3 = second_way(near_3)
+    swapped_2.append(swap(far_2))
+    swapped_3 = [swap(a) for a in (rest_unit, side_3, near_3)]
+    far_3, second_unit = together(far_3, second_unit)
+    near_4, side_4 = first_way(second_unit), second_way(second_unit)
+    swapped_3.append(swap(far_3))
+
+    units_1 = [near_unit, near_1, side_1, far_1]
+    units_2 = [first_unit, near_2, side_2, far_2]
+    units_3 = [rest_unit, near_3, side_3, far_3]
+    gate, up, down = w_gate[0], w_up[0], w_down[0]
+    is_owner = me == hot_expert
+    count_1, count_2, count_4 = 2 * message, (chips - 1) * message, chips * message
+    hot_plan = (
+        tuple((k, 0, count_1) for k in range(4))
+        + tuple((4 + k, 0, count_2) for k in range(4))
+        + tuple((8 + k, 0, count_2) for k in range(4))
+    )
+    flags = jnp.stack([core, is_owner.astype(jnp.int32), jnp.zeros((), jnp.int32)])
+    hot = expert_call(
+        flags,
+        (hot_plan,),
+        True,
+        chips,
+        units_1 + units_2 + units_3,
+        swapped_1 + swapped_2 + swapped_3,
+        gate,
+        up,
+        down,
+    )
+
+    on_owner_chip = hot_expert // 2 == chip
+    owned = []
+    for q in range(3):
+        kept, given = hot[2 * q], hot[2 * q + 1]
+        kept = jnp.where(is_owner, kept, swap(given))
+
+        def block(at, kept=kept):
+            return lax.dynamic_index_in_dim(
+                kept, jnp.clip(at, 0, chips - 1), 0, keepdims=False
+            )
+
+        upward = downward = None
+        for step in range(1, chips):
+            reach = chips - step
+            ups = [(j, j + 2) for j in range(0, 2 * step)]
+            downs = [(experts - 1 - j, experts - 3 - j) for j in range(0, 2 * step)]
+            sent_up, sent_down = block(chip + reach), block(chip - reach)
+            if step > 1:
+                sent_up = jnp.where(on_owner_chip, sent_up, upward)
+                sent_down = jnp.where(on_owner_chip, sent_down, downward)
+            upward = lax.ppermute(sent_up, "expert", ups)
+            downward = lax.ppermute(sent_down, "expert", downs)
+        arrived = jnp.where(hot_expert // 2 < chip, upward, downward)
+        owned.append(jnp.where(on_owner_chip, block(chip), arrived))
+    hot_grads = jnp.stack(owned, axis=1)
+
+    far_4 = second_way(near_4)
+    units_4 = [second_unit, near_4, side_4, far_4]
+    swapped_4 = [swap(a) for a in (second_unit, side_4, near_4, far_4)]
+    first_of_chip = jnp.where(on_owner_chip, hot_expert % 2, 0)
+    cold_plans = (
+        tuple((k, 0, message) for k in range(4)) + tuple((4 + k, 0, count_2) for k in range(4)),
+        tuple((8 + k, 0, message) for k in range(4))
+        + tuple((8 + k, message, count_2) for k in range(4)),
+    )
+    flags = jnp.stack(
+        [core, jnp.logical_not(is_owner).astype(jnp.int32), (first_of_chip != core).astype(jnp.int32)]
+    )
+    grad_gate, grad_up, grad_down = expert_call(
+        flags,
+        cold_plans,
+        False,
+        chips,
+        units_1 + units_2 + units_4,
+        swapped_1 + swapped_2 + swapped_4,
+        gate,
+        up,
+        down,
+    )
+    return (grad_gate[None], grad_up[None], grad_down[None], hot_grads[None])
+
+
 def solution(mesh):
     placed = (
         P(("dp", "expert"), None),

time: 341 us -> 292 us (0.86)
  starting transfers between devices: 6.88 us -> 122 us
  waiting for transfers between devices: 211 us -> 116 us
  blocking collectives: 52.2 us -> 0 us
  matrix products: 33.6 us -> 9.74 us
  Pallas kernels: 0 us -> 22.9 us
  between operations: 15.5 us -> 1.89 us
  other arithmetic: 14.8 us -> 8.66 us
    ppermute x0 -> x60, starting transfers between devices: none -> 122 us  [the longest x9 43.5 us: on_device(): upward = lax.ppermute(sent_up, 'expert', ups)]
    ppermute x0 -> x60, waiting for transfers between devices: none -> 116 us  [the longest x9 62 us: along(): lax.ppermute(array, 'expert', [(j, j ^ 2 * step) for j in range(experts)])]
    reduce_scatter x1 -> x0, waiting for transfers between devices: 92.6 us -> none  [on_device(): lax.psum_scatter(jnp.stack([gate_part, up_part, down_part], axis=1), 'exp...]
    psum x1 -> x0, waiting for transfers between devices: 71.2 us -> none  [spread(): return lax.psum(block, axis)]
    all_to_all x1 -> x0, blocking collectives: 52.2 us -> none  [on_device(): lax.all_to_all(send_grads, 'expert', split_axis=0, concat_axis=0, tiled=T...]
    all_to_all x1 -> x0, waiting for transfers between devices: 46.7 us -> none  [on_device(): lax.all_to_all(send_tokens, 'expert', split_axis=0, concat_axis=0, tiled=...]
    dot_general x12 -> x0, matrix products: 29.2 us -> none  [the longest x6 13.3 us: column_sum(): lax.dot_general(left, right, CONTRACT_ROWS, preferred_element_type=jnp.fl...]
    pallas_call x0 -> x6, Pallas kernels: none -> 22.9 us  [the longest x2 22.9 us: expert_call(): pl.pallas_call(kernel, out_shape=out_shape, in_specs=[pl.BlockSpec(memory...]
  transfers between devices with their start and end apart: 7 -> 60, of which waited for: 3 -> 24; matrix products, arithmetic and copies ran while one was open for 13% -> 7% of each run, Pallas kernels for 0% -> 1%
where the time goes in v1:
time: 292 us; the launch traced here: 291 us
  starting transfers between devices  122 us (42%)
  waiting for transfers between devices  116 us (40%)
  Pallas kernels  22.9 us (8%)
  matrix products  9.74 us (3%)
  local copies, waits for them, and re-layouts  9.68 us (3%)
  other arithmetic  8.66 us (3%)
    ppermute x9, waiting for transfers between devices, along(): lax.ppermute(array, 'expert', [(j, j ^ 2 * step) for j in range(experts)])  62 us
    ppermute x9, starting transfers between devices, on_device(): upward = lax.ppermute(sent_up, 'expert', ups)  43.5 us
    ppermute x21, starting transfers between devices, swap(): return lax.ppermute(array, 'expert', [(j, j ^ 1) for j in range(experts)])  38 us
    pallas_call x2, Pallas kernels, expert_call(): pl.pallas_call(kernel, out_shape=out_shape, in_specs=[pl.BlockSpec(memory...  22.9 us
    ppermute x9, waiting for transfers between devices, on_device(): upward = lax.ppermute(sent_up, 'expert', ups)  19.8 us
    ppermute x9, starting transfers between devices, along(): lax.ppermute(array, 'expert', [(j, j ^ 2 * step) for j in range(experts)])  19.1 us
    ppermute x8, waiting for transfers between devices, second_way(): return lax.ppermute(array, ('dp', 'expert'), pairs)  14 us
    ppermute x21, waiting for transfers between devices, swap(): return lax.ppermute(array, 'expert', [(j, j ^ 1) for j in range(experts)])  11.5 us
  transfers between devices with their start and end apart: 60, of which 24 were waited for; matrix products, arithmetic and copies ran while one was open for 7% of the time, Pallas kernels for 1%

profile of v1, /device:TPU:0, one launch (start us, length us, event | category | flops | bytes accessed | tf_op | source)
XLA Modules:
  0.0 290.9 jit_solution(8556077070130939014)
XLA Ops:
  7.0 4.8 %collective-permute-start.6 = (bf16[48,3584]{1,0:T(8,128)(2,1)S(1)}, bf16[48,3584]{1,0:T(8,128)(2,1)S(1)}, u32[]{:S(2)}, u32[]{:S(2)}) collective-permute-start(bf16[48,3584]{1,0:T(8,128)(2,1)S(1)} %convolution_convert_fusion.6), channel_id=1, source_target_pairs={{0,6},{1,7},{2,4},{3,5},{4,2},{5,3},{6,0},{7,1},{8,14},{9,15},{10,... | collective-permute-start | bytes 1032200 | tf_op jit(solution)/shard_map/ppermute | solution.py:332
  20.9 20.8 %collective-permute-done.5 = bf16[48,3584]{1,0:T(8,128)(2,1)S(1)} collective-permute-done((bf16[48,3584]{1,0:T(8,128)(2,1)S(1)}, bf16[48,3584]{1,0:T(8,128)(2,1)S(1)}, u32[]{:S(2)}, u32[]{:S(2)}) %collective-permute-start.5) | collective-permute-done | bytes 344096 | tf_op jit(solution)/shard_map/ppermute | solution.py:332
  48.9 3.0 %collective-permute-start.11 = (bf16[48,3584]{1,0:T(8,128)(2,1)S(1)}, bf16[48,3584]{1,0:T(8,128)(2,1)S(1)}, u32[]{:S(2)}, u32[]{:S(2)}) collective-permute-start(bf16[48,3584]{1,0:T(8,128)(2,1)S(1)} %copy-done.4), channel_id=1, source_target_pairs={{0,4},{1,5},{2,6},{3,7},{4,0},{5,1},{6,2},{7,3},{8,12},{9,13},{10,... | collective-permute-start | bytes 1032200 | tf_op jit(solution)/shard_map/ppermute | solution.py:332
  54.5 6.4 %collective-permute-done.10 = bf16[48,3584]{1,0:T(8,128)(2,1)S(1)} collective-permute-done((bf16[48,3584]{1,0:T(8,128)(2,1)}, bf16[48,3584]{1,0:T(8,128)(2,1)S(1)}, u32[]{:S(2)}, u32[]{:S(2)}) %collective-permute-start.10) | collective-permute-done | bytes 344096 | tf_op jit(solution)/shard_map/ppermute | solution.py:332
  62.5 13.2 %collective-permute-done.11 = bf16[48,3584]{1,0:T(8,128)(2,1)S(1)} collective-permute-done((bf16[48,3584]{1,0:T(8,128)(2,1)S(1)}, bf16[48,3584]{1,0:T(8,128)(2,1)S(1)}, u32[]{:S(2)}, u32[]{:S(2)}) %collective-permute-start.11) | collective-permute-done | bytes 344096 | tf_op jit(solution)/shard_map/ppermute | solution.py:332
  79.6 5.9 %collective-permute-start.16 = (bf16[48,3584]{1,0:T(8,128)(2,1)}, bf16[48,3584]{1,0:T(8,128)(2,1)S(1)}, u32[]{:S(2)}, u32[]{:S(2)}) collective-permute-start(bf16[48,3584]{1,0:T(8,128)(2,1)} %get-tuple-element.47), channel_id=1, source_target_pairs={{0,2},{1,3},{2,0},{3,1},{4,6},{5,7},{6,4},{7,5},{8,10},{9,11},{10,... | collective-permute-start | bytes 1032200 | tf_op jit(solution)/shard_map/ppermute | solution.py:332
  89.0 7.7 %collective-permute-done.16 = bf16[48,3584]{1,0:T(8,128)(2,1)S(1)} collective-permute-done((bf16[48,3584]{1,0:T(8,128)(2,1)}, bf16[48,3584]{1,0:T(8,128)(2,1)S(1)}, u32[]{:S(2)}, u32[]{:S(2)}) %collective-permute-start.16) | collective-permute-done | bytes 344096 | tf_op jit(solution)/shard_map/ppermute | solution.py:332
  100.9 13.3 %collective-permute-done.17 = bf16[48,3584]{1,0:T(8,128)(2,1)S(1)} collective-permute-done((bf16[48,3584]{1,0:T(8,128)(2,1)}, bf16[48,3584]{1,0:T(8,128)(2,1)S(1)}, u32[]{:S(2)}, u32[]{:S(2)}) %collective-permute-start.17) | collective-permute-done | bytes 344096 | tf_op jit(solution)/shard_map/ppermute | solution.py:332
  115.5 4.2 %collective-permute-done.13.refs_0_ = bf16[144,3584]{1,0:T(8,128)(2,1)} collective-permute-done((bf16[144,3584]{1,0:T(8,128)(2,1)}, bf16[144,3584]{1,0:T(8,128)(2,1)}, u32[]{:S(2)}, u32[]{:S(2)}) %collective-permute-start.13) | collective-permute-done | bytes 1032224 | tf_op jit(solution)/shard_map/ppermute | solution.py:340
  125.8 8.9 %collective-permute-done.19.refs_0_ = bf16[144,3584]{1,0:T(8,128)(2,1)S(1)} collective-permute-done((bf16[144,3584]{1,0:T(8,128)(2,1)}, bf16[144,3584]{1,0:T(8,128)(2,1)S(1)}, u32[]{:S(2)}, u32[]{:S(2)}) %collective-permute-start.19) | collective-permute-done | bytes 1032224 | tf_op jit(solution)/shard_map/ppermute | solution.py:340
  146.3 33.8 %collective-permute-start.39 = (bf16[4,448,256]{2,1,0:T(8,128)(2,1)}, bf16[4,448,256]{2,1,0:T(8,128)(2,1)S(1)}, u32[]{:S(2)}, u32[]{:S(2)}) collective-permute-start(bf16[4,448,256]{2,1,0:T(8,128)(2,1)} %get-tuple-element.61), channel_id=1, source_target_pairs={{0,1},{1,0},{2,3},{3,2},{4,5},{5,4},{6,7},{7,6},{8,9},{9,8},{10,11... | collective-permute-start | bytes 2752520 | tf_op jit(solution)/shard_map/ppermute | solution.py:329
  191.5 4.4 %collective-permute-start.54 = (bf16[448,256]{1,0:T(8,128)(2,1)S(1)}, bf16[448,256]{1,0:T(8,128)(2,1)S(1)}, u32[]{:S(2)}, u32[]{:S(2)}) collective-permute-start(bf16[448,256]{1,0:T(8,128)(2,1)S(1)} %get-tuple-element.82), channel_id=1, source_target_pairs={{0,2},{1,3},{8,10},{9,11},{16,18},{17,19},{24,26},{25,27}} | collective-permute-start | bytes 688136 | tf_op jit(solution)/shard_map/ppermute | solution.py:453
  199.5 13.4 %collective-permute-start.41 = (bf16[448,256]{1,0:T(8,128)(2,1)S(1)}, bf16[448,256]{1,0:T(8,128)(2,1)S(1)}, u32[]{:S(2)}, u32[]{:S(2)}) collective-permute-start(bf16[448,256]{1,0:T(8,128)(2,1)S(1)} %get-tuple-element.72), channel_id=1, source_target_pairs={{0,2},{1,3},{2,4},{3,5},{8,10},{9,11},{10,12},{11,13},{16,18},{17,... | collective-permute-start | bytes 688136 | tf_op jit(solution)/shard_map/ppermute | solution.py:453
  214.2 4.6 %collective-permute-start.48 = (bf16[448,256]{1,0:T(8,128)(2,1)S(1)}, bf16[448,256]{1,0:T(8,128)(2,1)S(1)}, u32[]{:S(2)}, u32[]{:S(2)}) collective-permute-start(bf16[448,256]{1,0:T(8,128)(2,1)S(1)} %get-tuple-element.76), channel_id=1, source_target_pairs={{0,2},{1,3},{2,4},{3,5},{8,10},{9,11},{10,12},{11,13},{16,18},{17,... | collective-permute-start | bytes 688136 | tf_op jit(solution)/shard_map/ppermute | solution.py:453
  223.7 7.3 %collective-permute-done.59 = bf16[448,256]{1,0:T(8,128)(2,1)S(1)} collective-permute-done((bf16[448,256]{1,0:T(8,128)(2,1)S(1)}, bf16[448,256]{1,0:T(8,128)(2,1)S(1)}, u32[]{:S(2)}, u32[]{:S(2)}) %collective-permute-start.59) | collective-permute-done | bytes 229408 | tf_op jit(solution)/shard_map/ppermute | solution.py:454
  231.0 3.6 %collective-permute-start.55 = (bf16[448,256]{1,0:T(8,128)(2,1)S(1)}, bf16[448,256]{1,0:T(8,128)(2,1)S(1)}, u32[]{:S(2)}, u32[]{:S(2)}) collective-permute-start(bf16[448,256]{1,0:T(8,128)(2,1)S(1)} %get-tuple-element.80), channel_id=1, source_target_pairs={{0,2},{1,3},{2,4},{3,5},{8,10},{9,11},{10,12},{11,13},{16,18},{17,... | collective-permute-start | bytes 688136 | tf_op jit(solution)/shard_map/ppermute | solution.py:453
  234.7 3.5 %collective-permute-done.55 = bf16[448,256]{1,0:T(8,128)(2,1)S(1)} collective-permute-done((bf16[448,256]{1,0:T(8,128)(2,1)S(1)}, bf16[448,256]{1,0:T(8,128)(2,1)S(1)}, u32[]{:S(2)}, u32[]{:S(2)}) %collective-permute-start.55) | collective-permute-done | bytes 229408 | tf_op jit(solution)/shard_map/ppermute | solution.py:453
  238.1 4.8 %collective-permute-start.42 = (bf16[448,256]{1,0:T(8,128)(2,1)S(1)}, bf16[448,256]{1,0:T(8,128)(2,1)S(1)}, u32[]{:S(2)}, u32[]{:S(2)}) collective-permute-start(bf16[448,256]{1,0:T(8,128)(2,1)S(1)} %bitcast_select_fusion.13), channel_id=1, source_target_pairs={{0,2},{1,3},{2,4},{3,5},{4,6},{5,7},{8,10},{9,11},{10,12},{11,13},... | collective-permute-start | bytes 688136 | tf_op jit(solution)/shard_map/ppermute | solution.py:453
  242.9 4.2 %collective-permute-done.42 = bf16[448,256]{1,0:T(8,128)(2,1)S(1)} collective-permute-done((bf16[448,256]{1,0:T(8,128)(2,1)S(1)}, bf16[448,256]{1,0:T(8,128)(2,1)S(1)}, u32[]{:S(2)}, u32[]{:S(2)}) %collective-permute-start.42) | collective-permute-done | bytes 229408 | tf_op jit(solution)/shard_map/ppermute | solution.py:453
  247.2 5.8 %collective-permute-start.49 = (bf16[448,256]{1,0:T(8,128)(2,1)S(1)}, bf16[448,256]{1,0:T(8,128)(2,1)S(1)}, u32[]{:S(2)}, u32[]{:S(2)}) collective-permute-start(bf16[448,256]{1,0:T(8,128)(2,1)S(1)} %bitcast_select_fusion.8), channel_id=1, source_target_pairs={{0,2},{1,3},{2,4},{3,5},{4,6},{5,7},{8,10},{9,11},{10,12},{11,13},... | collective-permute-start | bytes 688136 | tf_op jit(solution)/shard_map/ppermute | solution.py:453
  253.0 5.4 %collective-permute-done.49 = bf16[448,256]{1,0:T(8,128)(2,1)S(1)} collective-permute-done((bf16[448,256]{1,0:T(8,128)(2,1)S(1)}, bf16[448,256]{1,0:T(8,128)(2,1)S(1)}, u32[]{:S(2)}, u32[]{:S(2)}) %collective-permute-start.49) | collective-permute-done | bytes 229408 | tf_op jit(solution)/shard_map/ppermute | solution.py:453
  258.4 4.4 %collective-permute-start.56 = (bf16[448,256]{1,0:T(8,128)(2,1)S(1)}, bf16[448,256]{1,0:T(8,128)(2,1)S(1)}, u32[]{:S(2)}, u32[]{:S(2)}) collective-permute-start(bf16[448,256]{1,0:T(8,128)(2,1)S(1)} %bitcast_select_fusion.3), channel_id=1, source_target_pairs={{0,2},{1,3},{2,4},{3,5},{4,6},{5,7},{8,10},{9,11},{10,12},{11,13},... | collective-permute-start | bytes 688136 | tf_op jit(solution)/shard_map/ppermute | solution.py:453
  262.8 3.4 %collective-permute-done.56 = bf16[448,256]{1,0:T(8,128)(2,1)S(1)} collective-permute-done((bf16[448,256]{1,0:T(8,128)(2,1)S(1)}, bf16[448,256]{1,0:T(8,128)(2,1)S(1)}, u32[]{:S(2)}, u32[]{:S(2)}) %collective-permute-start.56) | collective-permute-done | bytes 229408 | tf_op jit(solution)/shard_map/ppermute | solution.py:453
  269.5 21.2 %cold_terms.1 = (bf16[3584,256]{1,0:T(8,128)(2,1)}, bf16[3584,256]{1,0:T(8,128)(2,1)}, bf16[256,3584]{1,0:T(8,128)(2,1)}) custom-call(s32[3]{0:T(128)} %pad_add_fusion.1.refs_0_, bf16[96,3584]{1,0:T(8,128)(2,1)} %get-tuple-element.35.refs_1_, bf16[96,3584]{1,0:T(8,128)(2,1)} %get-tuple-element.36.refs_2_, bf16[96,3584]{1,0:T(8,128)(2,1)} %get-tuple-element.37.refs_3_, ...), custom_call_target="tpu_custom_call" | custom-call | flops 8455716864 | bytes 22020096 | tf_op jit(solution)/shard_map/cold_terms/pallas_call | solution.py:280
  (208 shorter events, 81.0 us)
Async XLA Ops:
  13.5 28.3 %collective-permute-start.5 = (bf16[48,3584]{1,0:T(8,128)(2,1)S(1)}, bf16[48,3584]{1,0:T(8,128)(2,1)S(1)}, u32[]{:S(2)}, u32[]{:S(2)}) collective-permute-start(bf16[48,3584]{1,0:T(8,128)(2,1)S(1)} %convolution_convert_fusion.7), channel_id=1, source_target_pairs={{0,4},{1,5},{2,6},{3,7},{4,0},{5,1},{6,2},{7,3},{8,12},{9,13},{10,... | collective-permute-start | bytes 1032200 | tf_op jit(solution)/shard_map/ppermute | solution.py:332
  14.0 27.8 %collective-permute-start.4 = (bf16[48,3584]{1,0:T(8,128)(2,1)S(1)}, bf16[48,3584]{1,0:T(8,128)(2,1)S(1)}, u32[]{:S(2)}, u32[]{:S(2)}) collective-permute-start(bf16[48,3584]{1,0:T(8,128)(2,1)S(1)} %convolution_convert_fusion.8), channel_id=1, source_target_pairs={{0,2},{1,3},{2,0},{3,1},{4,6},{5,7},{6,4},{7,5},{8,10},{9,11},{10,... | collective-permute-start | bytes 1032200 | tf_op jit(solution)/shard_map/ppermute | solution.py:332
  15.1 27.6 %collective-permute-start.3 = (bf16[96,3584]{1,0:T(8,128)(2,1)S(1)}, bf16[96,3584]{1,0:T(8,128)(2,1)S(1)}, u32[]{:S(2)}, u32[]{:S(2)}) collective-permute-start(bf16[96,3584]{1,0:T(8,128)(2,1)S(1)} %convolution_convert_fusion.refs_0_), channel_id=1, source_target_pairs={{0,16},{1,9},{2,18},{3,11},{4,20},{5,13},{6,22},{7,15},{8,24},{9,1... | collective-permute-start | bytes 2064392 | tf_op jit(solution)/shard_map/ppermute | solution.py:340
  16.8 25.9 %collective-permute-start.2 = (bf16[96,3584]{1,0:T(8,128)(2,1)S(1)}, bf16[96,3584]{1,0:T(8,128)(2,1)}, u32[]{:S(2)}, u32[]{:S(2)}) collective-permute-start(bf16[96,3584]{1,0:T(8,128)(2,1)S(1)} %convolution_convert_fusion.refs_0_), channel_id=1, source_target_pairs={{0,8},{1,17},{2,10},{3,19},{4,12},{5,21},{6,14},{7,23},{8,0},{9,25... | collective-permute-start | bytes 2064392 | tf_op jit(solution)/shard_map/ppermute | solution.py:336
  43.6 33.1 %collective-permute-start.9 = (bf16[144,3584]{1,0:T(8,128)(2,1)}, bf16[144,3584]{1,0:T(8,128)(2,1)S(1)}, u32[]{:S(2)}, u32[]{:S(2)}) collective-permute-start(bf16[144,3584]{1,0:T(8,128)(2,1)} %get-tuple-element.38.refs_1_), channel_id=1, source_target_pairs={{0,16},{1,9},{2,18},{3,11},{4,20},{5,13},{6,22},{7,15},{8,24},{9,1... | collective-permute-start | bytes 3096584 | tf_op jit(solution)/shard_map/ppermute | solution.py:340
  45.1 32.5 %collective-permute-start.8 = (bf16[144,3584]{1,0:T(8,128)(2,1)}, bf16[144,3584]{1,0:T(8,128)(2,1)S(1)}, u32[]{:S(2)}, u32[]{:S(2)}) collective-permute-start(bf16[144,3584]{1,0:T(8,128)(2,1)} %get-tuple-element.38.refs_1_), channel_id=1, source_target_pairs={{0,8},{1,17},{2,10},{3,19},{4,12},{5,21},{6,14},{7,23},{8,0},{9,25... | collective-permute-start | bytes 3096584 | tf_op jit(solution)/shard_map/ppermute | solution.py:336
  48.9 26.8 %collective-permute-start.11 = (bf16[48,3584]{1,0:T(8,128)(2,1)S(1)}, bf16[48,3584]{1,0:T(8,128)(2,1)S(1)}, u32[]{:S(2)}, u32[]{:S(2)}) collective-permute-start(bf16[48,3584]{1,0:T(8,128)(2,1)S(1)} %copy-done.4), channel_id=1, source_target_pairs={{0,4},{1,5},{2,6},{3,7},{4,0},{5,1},{6,2},{7,3},{8,12},{9,13},{10,... | collective-permute-start | bytes 1032200 | tf_op jit(solution)/shard_map/ppermute | solution.py:332
  52.0 23.7 %collective-permute-start.12 = (bf16[48,3584]{1,0:T(8,128)(2,1)S(1)}, bf16[48,3584]{1,0:T(8,128)(2,1)S(1)}, u32[]{:S(2)}, u32[]{:S(2)}) collective-permute-start(bf16[48,3584]{1,0:T(8,128)(2,1)S(1)} %copy-done.5), channel_id=1, source_target_pairs={{0,6},{1,7},{2,4},{3,5},{4,2},{5,3},{6,0},{7,1},{8,14},{9,15},{10,... | collective-permute-start | bytes 1032200 | tf_op jit(solution)/shard_map/ppermute | solution.py:332
  85.5 29.9 %collective-permute-start.15 = (bf16[144,3584]{1,0:T(8,128)(2,1)}, bf16[144,3584]{1,0:T(8,128)(2,1)S(1)}, u32[]{:S(2)}, u32[]{:S(2)}) collective-permute-start(bf16[144,3584]{1,0:T(8,128)(2,1)} %get-tuple-element.46.refs_1_), channel_id=1, source_target_pairs={{0,16},{1,9},{2,18},{3,11},{4,20},{5,13},{6,22},{7,15},{8,24},{9,1... | collective-permute-start | bytes 3096584 | tf_op jit(solution)/shard_map/ppermute | solution.py:340
  86.1 29.4 %collective-permute-start.14 = (bf16[144,3584]{1,0:T(8,128)(2,1)}, bf16[144,3584]{1,0:T(8,128)(2,1)S(1)}, u32[]{:S(2)}, u32[]{:S(2)}) collective-permute-start(bf16[144,3584]{1,0:T(8,128)(2,1)} %get-tuple-element.46.refs_1_), channel_id=1, source_target_pairs={{0,8},{1,17},{2,10},{3,19},{4,12},{5,21},{6,14},{7,23},{8,0},{9,25... | collective-permute-start | bytes 3096584 | tf_op jit(solution)/shard_map/ppermute | solution.py:336
  86.6 33.2 %collective-permute-start.13 = (bf16[144,3584]{1,0:T(8,128)(2,1)}, bf16[144,3584]{1,0:T(8,128)(2,1)}, u32[]{:S(2)}, u32[]{:S(2)}) collective-permute-start(bf16[144,3584]{1,0:T(8,128)(2,1)} %get-tuple-element.44.refs_6_), channel_id=1, source_target_pairs={{0,16},{1,9},{2,18},{3,11},{4,20},{5,13},{6,22},{7,15},{8,24},{9,1... | collective-permute-start | bytes 3096584 | tf_op jit(solution)/shard_map/ppermute | solution.py:340
  88.1 26.1 %collective-permute-start.17 = (bf16[48,3584]{1,0:T(8,128)(2,1)}, bf16[48,3584]{1,0:T(8,128)(2,1)S(1)}, u32[]{:S(2)}, u32[]{:S(2)}) collective-permute-start(bf16[48,3584]{1,0:T(8,128)(2,1)} %get-tuple-element.48), channel_id=1, source_target_pairs={{0,4},{1,5},{2,6},{3,7},{4,0},{5,1},{6,2},{7,3},{8,12},{9,13},{10,... | collective-permute-start | bytes 1032200 | tf_op jit(solution)/shard_map/ppermute | solution.py:332
  140.1 41.6 %collective-permute-start.20 = (bf16[192,3584]{1,0:T(8,128)(2,1)}, bf16[192,3584]{1,0:T(8,128)(2,1)}, u32[]{:S(2)}, u32[]{:S(2)}) collective-permute-start(bf16[192,3584]{1,0:T(8,128)(2,1)} %get-tuple-element.53.refs_9_), channel_id=1, source_target_pairs={{0,8},{1,17},{2,10},{3,19},{4,12},{5,21},{6,14},{7,23},{8,0},{9,25... | collective-permute-start | bytes 4128776 | tf_op jit(solution)/shard_map/ppermute | solution.py:336
  146.3 36.9 %collective-permute-start.39 = (bf16[4,448,256]{2,1,0:T(8,128)(2,1)}, bf16[4,448,256]{2,1,0:T(8,128)(2,1)S(1)}, u32[]{:S(2)}, u32[]{:S(2)}) collective-permute-start(bf16[4,448,256]{2,1,0:T(8,128)(2,1)} %get-tuple-element.61), channel_id=1, source_target_pairs={{0,1},{1,0},{2,3},{3,2},{4,5},{5,4},{6,7},{7,6},{8,9},{9,8},{10,11... | collective-permute-start | bytes 2752520 | tf_op jit(solution)/shard_map/ppermute | solution.py:329
  181.2 18.3 %collective-permute-start.21 = (bf16[192,3584]{1,0:T(8,128)(2,1)S(1)}, bf16[192,3584]{1,0:T(8,128)(2,1)S(1)}, u32[]{:S(2)}, u32[]{:S(2)}) collective-permute-start(bf16[192,3584]{1,0:T(8,128)(2,1)S(1)} %copy-done), channel_id=1, source_target_pairs={{0,16},{1,9},{2,18},{3,11},{4,20},{5,13},{6,22},{7,15},{8,24},{9,1... | collective-permute-start | bytes 4128776 | tf_op jit(solution)/shard_map/ppermute | solution.py:340
  181.7 41.9 %collective-permute-start.22 = (bf16[192,3584]{1,0:T(8,128)(2,1)}, bf16[192,3584]{1,0:T(8,128)(2,1)S(1)}, u32[]{:S(2)}, u32[]{:S(2)}) collective-permute-start(bf16[192,3584]{1,0:T(8,128)(2,1)} %collective-permute-done.20.refs_10_), channel_id=1, source_target_pairs={{0,16},{1,9},{2,18},{3,11},{4,20},{5,13},{6,22},{7,15},{8,24},{9,1... | collective-permute-start | bytes 4128776 | tf_op jit(solution)/shard_map/ppermute | solution.py:340
  191.5 21.4 %collective-permute-start.54 = (bf16[448,256]{1,0:T(8,128)(2,1)S(1)}, bf16[448,256]{1,0:T(8,128)(2,1)S(1)}, u32[]{:S(2)}, u32[]{:S(2)}) collective-permute-start(bf16[448,256]{1,0:T(8,128)(2,1)S(1)} %get-tuple-element.82), channel_id=1, source_target_pairs={{0,2},{1,3},{8,10},{9,11},{16,18},{17,19},{24,26},{25,27}} | collective-permute-start | bytes 688136 | tf_op jit(solution)/shard_map/ppermute | solution.py:453
  196.6 17.6 %collective-permute-start.58 = (bf16[448,256]{1,0:T(8,128)(2,1)S(1)}, bf16[448,256]{1,0:T(8,128)(2,1)S(1)}, u32[]{:S(2)}, u32[]{:S(2)}) collective-permute-start(bf16[448,256]{1,0:T(8,128)(2,1)S(1)} %bitcast_select_fusion), channel_id=1, source_target_pairs={{7,5},{6,4},{5,3},{4,2},{15,13},{14,12},{13,11},{12,10},{23,21},{2... | collective-permute-start | bytes 688136 | tf_op jit(solution)/shard_map/ppermute | solution.py:454
  197.3 21.5 %collective-permute-start.45 = (bf16[448,256]{1,0:T(8,128)(2,1)S(1)}, bf16[448,256]{1,0:T(8,128)(2,1)S(1)}, u32[]{:S(2)}, u32[]{:S(2)}) collective-permute-start(bf16[448,256]{1,0:T(8,128)(2,1)S(1)} %get-tuple-element.71), channel_id=1, source_target_pairs={{7,5},{6,4},{5,3},{4,2},{3,1},{2,0},{15,13},{14,12},{13,11},{12,10... | collective-permute-start | bytes 688136 | tf_op jit(solution)/shard_map/ppermute | solution.py:454
  199.5 19.4 %collective-permute-start.41 = (bf16[448,256]{1,0:T(8,128)(2,1)S(1)}, bf16[448,256]{1,0:T(8,128)(2,1)S(1)}, u32[]{:S(2)}, u32[]{:S(2)}) collective-permute-start(bf16[448,256]{1,0:T(8,128)(2,1)S(1)} %get-tuple-element.72), channel_id=1, source_target_pairs={{0,2},{1,3},{2,4},{3,5},{8,10},{9,11},{10,12},{11,13},{16,18},{17,... | collective-permute-start | bytes 688136 | tf_op jit(solution)/shard_map/ppermute | solution.py:453
  218.8 48.4 %collective-permute-start.31 = (bf16[192,3584]{1,0:T(8,128)(2,1)S(1)}, bf16[192,3584]{1,0:T(8,128)(2,1)S(1)}, u32[]{:S(2)}, u32[]{:S(2)}) collective-permute-start(bf16[192,3584]{1,0:T(8,128)(2,1)S(1)} %copy-done), channel_id=1, source_target_pairs={{0,1},{1,0},{2,3},{3,2},{4,5},{5,4},{6,7},{7,6},{8,9},{9,8},{10,11... | collective-permute-start | bytes 4128776 | tf_op jit(solution)/shard_map/ppermute | solution.py:329
  218.9 48.3 %collective-permute-start.33 = (bf16[192,3584]{1,0:T(8,128)(2,1)}, bf16[192,3584]{1,0:T(8,128)(2,1)S(1)}, u32[]{:S(2)}, u32[]{:S(2)}) collective-permute-start(bf16[192,3584]{1,0:T(8,128)(2,1)} %collective-permute-done.20.refs_10_), channel_id=1, source_target_pairs={{0,1},{1,0},{2,3},{3,2},{4,5},{5,4},{6,7},{7,6},{8,9},{9,8},{10,11... | collective-permute-start | bytes 4128776 | tf_op jit(solution)/shard_map/ppermute | solution.py:329
  220.8 46.5 %collective-permute-start.32 = (bf16[192,3584]{1,0:T(8,128)(2,1)S(1)}, bf16[192,3584]{1,0:T(8,128)(2,1)S(1)}, u32[]{:S(2)}, u32[]{:S(2)}) collective-permute-start(bf16[192,3584]{1,0:T(8,128)(2,1)S(1)} %collective-permute-done.21.refs_11_), channel_id=1, source_target_pairs={{0,1},{1,0},{2,3},{3,2},{4,5},{5,4},{6,7},{7,6},{8,9},{9,8},{10,11... | collective-permute-start | bytes 4128776 | tf_op jit(solution)/shard_map/ppermute | solution.py:329
  223.6 44.8 %collective-permute-start.34 = (bf16[192,3584]{1,0:T(8,128)(2,1)S(1)}, bf16[192,3584]{1,0:T(8,128)(2,1)}, u32[]{:S(2)}, u32[]{:S(2)}) collective-permute-start(bf16[192,3584]{1,0:T(8,128)(2,1)S(1)} %collective-permute-done.22.refs_12_), channel_id=1, source_target_pairs={{0,1},{1,0},{2,3},{3,2},{4,5},{5,4},{6,7},{7,6},{8,9},{9,8},{10,11... | collective-permute-start | bytes 4128776 | tf_op jit(solution)/shard_map/ppermute | solution.py:329
  (66 other events, 615.6 us)
